TPU v7x, 512 devices: a whole 4x8x8 slice. The times are simulated.
512 devices in a mesh: batch: 2 (over core), token: 32 (over x, z), hidden: 8 (over y).
Axes of the slice: x: 4, y: 8, z: 8, core: 2. Of those that a mesh axis runs over, the one named last changes fastest.
Arguments:
- hist_len: int32 [512], replicated, may hold values from 32 to 512, as said below
- queries: bfloat16 [32, 1536], P(None, 'token'), may hold values from -4 to 4
- history_keys: bfloat16 [1536, 1536, 128], P(('batch', 'hidden'), 'token'), may hold values from -192 to 192
- cached_history_values: bfloat16 [1536, 1536, 128], P(('batch', 'hidden'), 'token'), may hold values from -6 to 6
- gain_mix: float32 [1536], replicated, may hold values from 0.25 to 1.75
- w_up: bfloat16 [32, 1536, 3072], P('token', None, 'hidden'), may hold values from -0.15625 to 0.15625
- w_down: bfloat16 [32, 3072, 1536], P('token', 'hidden'), may hold values from -0.109375 to 0.109375
- gain_out: float32 [1536], replicated, may hold values from 0.25 to 1.75
Outputs:
- mixer_out: bfloat16 [512, 32, 1536], P(('batch', 'hidden'), 'token')
Inputs may be any that keep to these rules, and one draw needn't show every extreme that they name: `hist_len`: along batch+hidden, the requests of each index need between 32 and 96 slots, indices 2i and 2i + 1 need 4 * 32 slots together, and some index needs exactly 96; within an index, requests 2j and 2j + 1 need from 2 to 6 slots together.
All inputs are finite; a program needn't handle non-finite values.
Results may differ from a plain program's by a relative error of at most 0.015.
Values may be sent and summed in bfloat16 or wider, within the bound.
A program may use at most 64 MiB of HBM per device.

v0:
```python
import jax
import jax.numpy as jnp
from jax import lax
from jax.sharding import PartitionSpec as P

TOKEN_COUNT = 32
MODEL_WIDTH = 1536
BLOCK_POSITIONS = 128
REQ_DEV = 32


EPSILON = 1e-05
NEGATIVE_FILL = -1e30


def in_blocks(x, dim, length):
    dims = x.shape
    parts = x.reshape(*dims[:dim], length, dims[dim] // length, *dims[dim + 1 :])
    return jnp.moveaxis(parts, dim, 0)


def sent_and_summed(x, axis, dim):
    length = lax.axis_size(axis)
    parts = lax.all_to_all(in_blocks(x, dim, length), axis, 0, 0, tiled=True)
    return jnp.sum(parts.astype(jnp.float32), axis=0)


def slot_layout(lengths, slot_count, block_rows):
    request_count = lengths.shape[0]
    blocks = (lengths + block_rows - 1) // block_rows
    block_ends = jnp.cumsum(blocks)
    block_starts = block_ends - blocks
    slot_index = jnp.arange(slot_count, dtype=jnp.int32)
    owners = jnp.sum((block_ends[None, :] <= slot_index[:, None]).astype(jnp.int32), axis=1)
    onehot = owners[:, None] == jnp.arange(request_count, dtype=jnp.int32)[None, :]
    start_of = jnp.sum(jnp.where(onehot, block_starts[None, :], 0), axis=1)
    length_of = jnp.sum(jnp.where(onehot, lengths[None, :], 0), axis=1)
    valid_rows = jnp.clip(length_of - (slot_index - start_of) * block_rows, 0, block_rows)
    return (onehot, valid_rows)


def block_partials(query_heads, slot_keys, slot_values, valid_rows, score_scale):
    scores = (
        jnp.einsum("qhs,nhsp->nqhp", query_heads, slot_keys, preferred_element_type=jnp.float32)
        * score_scale
    )
    position = jnp.arange(slot_keys.shape[-1], dtype=jnp.int32)
    in_range = position[None, None, None, :] < valid_rows[:, None, None, None]
    scores = jnp.where(in_range, scores, NEGATIVE_FILL)
    maxima = jnp.max(scores, axis=-1)
    softmax_terms = jnp.where(in_range, jnp.exp(scores - maxima[..., None]), 0.0)
    totals = jnp.sum(softmax_terms, axis=-1)
    weighted = jnp.einsum(
        "nqhp,nhsp->nqhs",
        softmax_terms.astype(jnp.bfloat16),
        slot_values,
        preferred_element_type=jnp.float32,
    )
    return (maxima, totals, weighted)


def combine_blocks(maxima, totals, weighted, onehot):
    owned = onehot.astype(jnp.float32)
    is_live = jnp.sum(owned, axis=1) > 0.5
    masked_max = jnp.where(onehot[:, :, None, None], maxima[:, None, :, :], NEGATIVE_FILL)
    request_max = jnp.max(masked_max, axis=0)
    owner_max = jnp.einsum("nr,rqh->nqh", owned, request_max, precision=lax.Precision.HIGHEST)
    factor = jnp.exp(jnp.where(is_live[:, None, None], maxima - owner_max, NEGATIVE_FILL))
    denominator = jnp.einsum("nr,nqh->rqh", owned, factor * totals, precision=lax.Precision.HIGHEST)
    numerator = jnp.einsum(
        "nr,nqhs->rqhs", owned, factor[..., None] * weighted, precision=lax.Precision.HIGHEST
    )
    return (numerator / denominator[..., None]).astype(jnp.bfloat16)


def layer_norm(summand):
    average = jnp.mean(summand, axis=-1, keepdims=True)
    centred = summand - average
    variance = jnp.mean(centred * centred, axis=-1, keepdims=True)
    return centred * lax.rsqrt(variance + EPSILON)


def local(hist_len, queries, history_keys, cached_history_values, gain_mix, w_up, w_down, gain_out):
    group_size = lax.axis_size(("batch", "hidden"))
    my_index = lax.axis_index(("batch", "hidden"))
    head_size = MODEL_WIDTH // TOKEN_COUNT
    local_heads = history_keys.shape[1] // head_size
    slot_count = history_keys.shape[0]
    score_scale = head_size ** (-0.5)
    query_heads = queries.reshape(TOKEN_COUNT, local_heads, head_size)
    all_lengths = hist_len.reshape(group_size, REQ_DEV)
    peer_ids = jnp.arange(group_size, dtype=jnp.int32)
    mine_hot = peer_ids == my_index
    own_lengths = jnp.sum(jnp.where(mine_hot[:, None], all_lengths, 0), axis=0)
    onehot, valid_rows = slot_layout(own_lengths, slot_count, BLOCK_POSITIONS)
    slot_keys = history_keys.reshape(slot_count, local_heads, head_size, BLOCK_POSITIONS)
    slot_values = cached_history_values.reshape(slot_count, local_heads, head_size, BLOCK_POSITIONS)
    maxima, totals, weighted = block_partials(
        query_heads, slot_keys, slot_values, valid_rows, score_scale
    )
    attended = combine_blocks(maxima, totals, weighted, onehot)
    unmixed = lax.all_to_all(
        attended.reshape(REQ_DEV, TOKEN_COUNT, local_heads * head_size),
        "token",
        split_axis=1,
        concat_axis=2,
        tiled=True,
    )
    mixed_rows = jnp.transpose(attended, (0, 2, 1, 3)).reshape(
        REQ_DEV, local_heads, TOKEN_COUNT * head_size
    )
    joined = mixed_rows.astype(jnp.float32) + unmixed.astype(jnp.float32)
    normed = (layer_norm(joined) * gain_mix).astype(jnp.bfloat16)
    lifted = jnp.einsum(
        "ntd,tdf->ntf",
        lax.all_gather(normed, "hidden", axis=0, tiled=True),
        w_up,
        preferred_element_type=jnp.float32,
    )
    activated = jax.nn.gelu(lifted, approximate=False).astype(jnp.bfloat16)
    partial_sums = jnp.einsum("ntf,tfd->ntd", activated, w_down, preferred_element_type=jnp.float32)
    summed = sent_and_summed(partial_sums.astype(jnp.bfloat16), "hidden", 0)
    return (layer_norm(summed + normed.astype(jnp.float32)) * gain_out).astype(jnp.bfloat16)


def solution(mesh):
    return jax.shard_map(
        local,
        mesh=mesh,
        in_specs=(
            P(),
            P(None, "token"),
            P(("batch", "hidden"), "token", None),
            P(("batch", "hidden"), "token", None),
            P(),
            P("token", None, "hidden"),
            P("token", "hidden", None),
            P(),
        ),
        out_specs=P(("batch", "hidden"), "token", None),
        check_vma=False,
    )
```

profile of v0, /device:TPU:2, one launch (start us, length us, event | category | flops | bytes accessed | tf_op | source)
XLA Modules:
  0.0 88.5 jit_solution(1204152583943687451)
XLA Ops:
  0.0 0.0 copy-start
  0.0 0.9 reshape.733
  0.9 0.1 select_reduce_fusion.3
  1.0 0.1 copy.35
  1.1 0.1 reduce-window.7
  1.1 0.1 reduce.12
  1.2 0.1 convert_reduce_fusion.2
  1.4 0.1 select_reduce_fusion.1
  1.5 0.1 iota_compare_fusion
  1.6 0.0 copy-done
  1.6 1.3 %bitcast_reduce_fusion = (f32[96,32]{1,0:T(8,128)S(1)}, f32[1,96,128,32]{2,3,1,0:T(8,128)S(1)}) fusion(bf16[96,48,128]{2,1,0:T(8,128)(2,1)S(1)} %copy-done, bf16[32,48]{1,0:T(8,128)(2,1)} %param.9, pred[96,128]{1,0:T(8,128)(4,1)S(1)} %iota_compare_fusion), kind=kOutput, calls=%fused_computation.4 | convolution fusion | flops 38925312 | bytes 2780160 | tf_op jit(solution)/shard_map/qhs,nhsp->nqhp/dot_general | solution.py:44
  2.9 0.1 copy.37
  3.0 1.0 %fusion.5 = f32[96,32]{1,0:T(8,128)S(1)} fusion(f32[1,96,128,32]{2,3,1,0:T(8,128)S(1)} %get-tuple-element.10, f32[96,32]{1,0:T(8,128)S(1)} %get-tuple-element.9, pred[96,128]{1,0:T(8,128)(4,1)S(1)} %iota_compare_fusion), kind=kLoop, calls=%fused_computation.11 | loop fusion | flops 1176576 | bytes 1609728 | tf_op jit(solution)/shard_map/reduce_sum | solution.py:52
  4.0 0.1 copy.40
  4.0 0.2 select_reduce_fusion
  4.3 0.2 fusion.17
  4.5 0.1 copy.38
  4.6 0.1 fusion.83
  4.7 2.1 %fusion = f32[96,32,48]{2,1,0:T(8,128)S(1)} fusion(bf16[96,48,128]{2,1,0:T(8,128)(2,1)} %param.11, f32[1,96,128,32]{2,3,1,0:T(8,128)S(1)} %get-tuple-element.10, f32[96,32]{1,0:T(8,128)S(1)} %get-tuple-element.9, f32[96,32]{1,0:T(8,128)S(1)} %copy.38, pred[96,128]{1,0:T(8,128)(4,1)S(1)} %iota_compare_fusion), kind=kOutput, calls=%fused_computation.2 | convolution fusion | flops 39075840 | bytes 3379200 | tf_op jit(solution)/shard_map/nqhp,nhsp->nqhs/dot_general | solution.py:53
  6.8 1.6 %fusion.10 = bf16[32,32,48]{2,0,1:T(8,128)(2,1)S(1)} fusion(f32[96,32,48]{2,1,0:T(8,128)S(1)} %fusion, f32[32,32]{0,1:T(8,128)S(1)} %fusion.83, s32[96]{0:T(128)S(1)} %convert_reduce_fusion.2), kind=kOutput, calls=%fused_computation.14 | convolution fusion | flops 56724480 | bytes 692608 | tf_op jit(solution)/shard_map/nr,nqhs->rqhs/dot_general | solution.py:70
  8.4 0.4 reshape.745
  8.7 22.2 %all_to_all.14 = bf16[32,2,768]{2,1,0:T(2,128)(2,1)S(1)} all-to-all(bf16[32,2,768]{2,1,0:T(2,128)(2,1)S(1)} %reshape.745), channel_id=1, replica_groups=mesh['batch'=2,'token'=32,'hidden'=8] {'token'}, dimensions={0} | all-to-all | bytes 196608 | tf_op jit(solution)/shard_map/all_to_all | solution.py:102
  31.0 0.2 reshape.746
  31.2 0.0 copy-start.1
  31.2 0.2 fusion.123
  31.5 0.3 copy.42
  31.8 0.3 add.108
  32.0 0.2 multiply_reduce_fusion.1
  32.3 0.0 copy-done.1
  32.3 0.1 multiply_convert_fusion.2
  32.4 27.8 %all_gather.3 = bf16[256,1,1536]{2,0,1:T(8,128)(2,1)S(1)} all-gather(bf16[32,1,1536]{2,0,1:T(8,128)(2,1)S(1)} %multiply_convert_fusion.2), channel_id=1, replica_groups=mesh['batch'=2,'token'=32,'hidden'=8] {'hidden'}, dimensions={0}, use_global_device_ids=true | all-gather | bytes 884736 | tf_op jit(solution)/shard_map/all_gather | solution.py:116
  60.2 4.4 %convolution_convert_fusion = bf16[256,1536]{1,0:T(8,128)(2,1)} fusion(bf16[1,384,1536]{2,1,0:T(8,128)(2,1)} %param.14, bf16[1,1536,384]{2,1,0:T(8,128)(2,1)} %param.13, bf16[256,1,1536]{2,0,1:T(8,128)(2,1)S(1)} %all_gather.3), kind=kOutput, calls=%fused_computation | convolution fusion | flops 610762752 | bytes 3932160 | tf_op jit(solution)/shard_map/ntf,tfd->ntd/dot_general | solution.py:121
  64.6 5.2 %all-to-all-start.1 = ((bf16[8,32,1,1536]{3,1,2,0:T(8,128)(2,1)}), bf16[8,32,1,1536]{3,1,2,0:T(8,128)(2,1)S(1)}, u32[]{:S(2)}, u32[]{:S(2)}) async-start(bf16[8,32,1,1536]{3,1,2,0:T(8,128)(2,1)} %bitcast.162), calls=%async_computation.1 | async-start | bytes 1572864 | tf_op jit(solution)/shard_map/all_to_all | solution.py:24
  69.8 0.1 mul.216
  69.9 0.0 copy-start.2
  69.9 16.8 %all-to-all-done.1 = bf16[8,32,1,1536]{3,1,2,0:T(8,128)(2,1)S(1)} async-done(((bf16[8,32,1,1536]{3,1,2,0:T(8,128)(2,1)}), bf16[8,32,1,1536]{3,1,2,0:T(8,128)(2,1)S(1)}, u32[]{:S(2)}, u32[]{:S(2)}) %all-to-all-start.1) | async-done | bytes 786464 | tf_op jit(solution)/shard_map/all_to_all | solution.py:24
  86.7 0.1 convert_reduce_fusion
  86.8 0.2 reduce_sum.113
  87.0 0.5 fusion.24
  87.5 0.2 multiply_reduce_fusion
  87.7 0.0 copy-done.2
  87.7 0.8 multiply_convert_fusion.1
  (11 shorter events, 0.1 us)
Async XLA Ops:
  0.0 1.6 %copy-start = (bf16[96,48,128]{2,1,0:T(8,128)(2,1)S(1)}, bf16[96,48,128]{2,1,0:T(8,128)(2,1)}, u32[]{:S(2)}) copy-start(bf16[96,48,128]{2,1,0:T(8,128)(2,1)} %param.10) | copy-start | bytes 3538948
  31.2 1.0 %copy-start.1 = (f32[1536]{0:T(1024)S(1)}, f32[1536]{0:T(1024)}, u32[]{:S(2)}) copy-start(f32[1536]{0:T(1024)} %param.12) | copy-start | bytes 18436
  64.6 22.1 %all-to-all-start.1 = ((bf16[8,32,1,1536]{3,1,2,0:T(8,128)(2,1)}), bf16[8,32,1,1536]{3,1,2,0:T(8,128)(2,1)S(1)}, u32[]{:S(2)}, u32[]{:S(2)}) async-start(bf16[8,32,1,1536]{3,1,2,0:T(8,128)(2,1)} %bitcast.162), calls=%async_computation.1 | async-start | bytes 1572864 | tf_op jit(solution)/shard_map/all_to_all | solution.py:24
  69.9 17.8 %copy-start.2 = (f32[1536]{0:T(1024)S(1)}, f32[1536]{0:T(1024)}, u32[]{:S(2)}) copy-start(f32[1536]{0:T(1024)} %param.15) | copy-start | bytes 18436
where the time goes:
time: 88.8 us; the launch traced here: 88.5 us
  blocking collectives  50.1 us (56%)
  waiting for transfers between devices  16.8 us (19%)
  matrix products  9.73 us (11%)
  starting transfers between devices  5.24 us (6%)
  other arithmetic  3.89 us (4%)
  local copies, waits for them, and re-layouts  2.65 us (3%)
    all_gather x1, blocking collectives, local(): lax.all_gather(normed, 'hidden', axis=0, tiled=True)  27.8 us
    all_to_all x1, blocking collectives, local(): lax.all_to_all(attended.reshape(REQ_DEV, TOKEN_COUNT, local_heads * head_...  22.2 us
    all_to_all x1, waiting for transfers between devices, sent_and_summed(): parts = lax.all_to_all(in_blocks(x, dim, length), axis, 0, 0, tiled=True)  16.8 us
    all_to_all x1, starting transfers between devices, sent_and_summed(): parts = lax.all_to_all(in_blocks(x, dim, length), axis, 0, 0, tiled=True)  5.24 us
    dot_general x1, matrix products, local(): jnp.einsum('ntf,tfd->ntd', activated, w_down, preferred_element_type=jnp....  4.37 us
    dot_general x1, matrix products, block_partials(): jnp.einsum('nqhp,nhsp->nqhs', softmax_terms.astype(jnp.bfloat16), slot_va...  2.12 us
  transfers between devices with their start and end apart: 1, of which 1 were waited for; matrix products, arithmetic and copies ran while one was open for 0% of the time, Pallas kernels for 0%

commit v1 on v0

v1 whole, which is shorter than its diff:
```python
import functools
import math

import jax
import jax.numpy as jnp
from jax import lax
from jax.experimental import pallas as pl
from jax.experimental.pallas import tpu as pltpu
from jax.sharding import PartitionSpec as P

TOKENS = 32
WIDTH = 1536
HEAD = 48
POS = 128
REQ_DEV = 32
SLOTS = 96
RING = 8
HALVES = 2
ROWS = REQ_DEV // HALVES
PAIR_SLOTS = 6
PAIRS = ROWS // 2
UNROLL = 4
MID = WIDTH // 2
FILL = -1e30
EPSILON = 1e-5
MESH = pl.DeviceIdType.MESH


def layer_norm(x):
    mean = jnp.sum(x, axis=-1, keepdims=True) * (1.0 / WIDTH)
    c = x - mean
    var = jnp.sum(c * c, axis=-1, keepdims=True) * (1.0 / WIDTH)
    return c * lax.rsqrt(var + EPSILON)


def kernel(
    len_ref, q_ref, gain_ref, k_hbm, v_hbm, up_hbm, down_hbm,
    out_ref,
    k_ref, v_ref, up_ref, down_ref, att, tiles, others, rows, part, out_buf, in_buf,
    load_sem, a2a_send, a2a_recv, ag_send, ag_recv, rs_send, rs_recv,
):
    me = lax.axis_index("token")
    y = lax.axis_index("hidden")
    group = lax.axis_index("batch") * RING + y
    above, below = lax.rem(y + 1, RING), lax.rem(y + RING - 1, RING)

    loads = [
        pltpu.make_async_copy(k_hbm, k_ref, load_sem.at[0]),
        pltpu.make_async_copy(v_hbm, v_ref, load_sem.at[1]),
        pltpu.make_async_copy(up_hbm.at[0], up_ref, load_sem.at[2]),
        pltpu.make_async_copy(down_hbm.at[0], down_ref, load_sem.at[3]),
    ]
    for load in loads:
        load.start()

    barrier = pltpu.get_barrier_semaphore()

    def greet(i, c):
        pl.semaphore_signal(
            barrier, inc=1, device_id={"token": lax.rem(me + i, TOKENS)}, device_id_type=MESH
        )
        return c

    lax.fori_loop(1, TOKENS, greet, 0)
    for near in (above, below):
        pl.semaphore_signal(barrier, inc=1, device_id={"hidden": near}, device_id_type=MESH)

    att[...] = jnp.zeros_like(att)
    position = lax.broadcasted_iota(jnp.int32, (1, PAIR_SLOTS * POS), 1)
    scale = HEAD ** -0.5
    loads[0].wait()
    loads[1].wait()

    def attend_pair(pair, start, half):
        request = group * REQ_DEV + half * ROWS + pair * 2
        len_a, len_b = len_ref[request], len_ref[request + 1]
        used_a = lax.shift_right_logical(len_a + (POS - 1), 7)
        used_b = lax.shift_right_logical(len_b + (POS - 1), 7)
        slot = [jnp.minimum(start + i, SLOTS - 1) for i in range(PAIR_SLOTS)]
        keys = jnp.concatenate([k_ref[s] for s in slot], axis=1)
        values = jnp.concatenate([v_ref[s] for s in slot], axis=1)
        score = jnp.dot(q_ref[...], keys, preferred_element_type=jnp.float32) * scale
        edge = used_a * POS
        of_a = position < edge
        in_a = position < len_a
        in_b = jnp.logical_and(position >= edge, position < edge + len_b)
        max_a = jnp.max(jnp.where(in_a, score, FILL), axis=1, keepdims=True)
        max_b = jnp.max(jnp.where(in_b, score, FILL), axis=1, keepdims=True)
        term = jnp.exp(score - jnp.where(of_a, max_a, max_b))
        term_a = jnp.where(in_a, term, 0.0)
        term_b = jnp.where(in_b, term, 0.0)
        both = jnp.concatenate([term_a, term_b], axis=0)
        total = jnp.sum(both, axis=1, keepdims=True)
        acc = lax.dot_general(
            both.astype(jnp.bfloat16), values, (((1,), (1,)), ((), ())),
            preferred_element_type=jnp.float32,
        )
        row = pl.multiple_of(pair * (2 * TOKENS), 2 * TOKENS)
        att[pl.ds(row, 2 * TOKENS), 0:HEAD] = acc / total
        return start + used_a + used_b

    def attend(half, start):
        def step(i, start):
            for u in range(UNROLL):
                start = attend_pair(i * UNROLL + u, start, half)
            return start

        start = lax.fori_loop(0, PAIRS // UNROLL, step, start)
        for q in range(TOKENS):
            tiles[half, q] = att[pl.ds(q, ROWS, stride=TOKENS), :].astype(jnp.bfloat16)
        others[half, me] = tiles[half, me]
        return start

    def exchange(half):
        def send(i, c):
            to = lax.rem(me + i, TOKENS)
            pltpu.make_async_remote_copy(
                src_ref=tiles.at[half, to],
                dst_ref=others.at[half, me],
                send_sem=a2a_send.at[half],
                recv_sem=a2a_recv.at[half],
                device_id={"token": to},
                device_id_type=MESH,
            ).start()
            return c

        lax.fori_loop(1, TOKENS, send, 0)

    def all_tiles(ref, half, sem):
        some = ref.at[half, pl.ds(0, TOKENS - 1)]
        return pltpu.make_async_copy(some, some, sem.at[half])

    lane = lax.broadcasted_iota(jnp.int32, (ROWS, 128), 1)

    def mix(half):
        all_tiles(others, half, a2a_recv).wait()
        out = [None] * (WIDTH // 128)
        for j in range(TOKENS):
            x = tiles[half, j].astype(jnp.float32) + others[half, j].astype(jnp.float32)
            first = j * HEAD
            shift = first % 128
            if shift:
                x = pltpu.roll(x, shift, 1)
            t = first // 128
            if shift + HEAD > 128:
                out[t] = jnp.where(lane >= shift, x, out[t])
                out[t + 1] = x
            else:
                out[t] = x if out[t] is None else jnp.where(lane >= shift, x, out[t])
        normed = layer_norm(jnp.concatenate(out, axis=1)) * gain_ref[0:1, :]
        rows[half, y] = normed.astype(jnp.bfloat16)

    LOW, HIGH, ALL = pl.ds(0, MID), pl.ds(MID, MID), pl.ds(0, WIDTH)

    def gather(half, way, hop):
        to = (above, below)[way]
        back = hop - 1
        source = lax.rem(y + (RING - back if way == 0 else back), RING)
        cols = ALL if hop < 4 else (LOW, HIGH)[way]
        block = rows.at[half, source, :, cols]
        return pltpu.make_async_remote_copy(
            src_ref=block, dst_ref=block,
            send_sem=ag_send.at[half, way, hop - 1], recv_sem=ag_recv.at[half, way, hop - 1],
            device_id={"hidden": to}, device_id_type=MESH,
        )

    def arrived(half, way, hop):
        source = lax.rem(y + (RING - hop if way == 0 else hop), RING)
        cols = ALL if hop < 4 else (LOW, HIGH)[way]
        block = rows.at[half, source, :, cols]
        return pltpu.make_async_remote_copy(
            src_ref=block, dst_ref=block,
            send_sem=ag_send.at[half, way, hop - 1], recv_sem=ag_recv.at[half, way, hop - 1],
            device_id={"hidden": (below, above)[way]}, device_id_type=MESH,
        )

    def forward(half, hop):
        for way in range(2):
            arrived(half, way, hop).wait_recv()
            if hop < 4:
                gather(half, way, hop + 1).start()

    ORDER = [0, RING - 1, 1, RING - 2, 2, RING - 3, 3, 4]

    def ffn(half, first, last):
        x = jnp.concatenate(
            [rows[half, lax.rem(y + ORDER[i], RING)] for i in range(first, last)], axis=0
        )
        up = jnp.dot(x, up_ref[...], preferred_element_type=jnp.float32)
        act = (0.5 * up * (1.0 + lax.erf(up * math.sqrt(0.5)))).astype(jnp.bfloat16)
        down = jnp.dot(act, down_ref[...], preferred_element_type=jnp.float32)
        part[half, first:last] = down.reshape(last - first, ROWS, WIDTH)

    def sums(half, way, step):
        cols = ALL if step else (LOW, HIGH)[way]
        return pltpu.make_async_remote_copy(
            src_ref=out_buf.at[half, way, step, :, cols],
            dst_ref=in_buf.at[half, way, step, :, cols],
            send_sem=rs_send.at[half, way, step], recv_sem=rs_recv.at[half, way, step],
            device_id={"hidden": (below, above)[way]}, device_id_type=MESH,
        )

    def scatter(half, step):
        d = 4 - step
        for way in range(2):
            if step == 0:
                cols = (slice(0, MID), slice(MID, WIDTH))[way]
                out_buf[half, way, 0, :, cols] = part[half, 7, :, cols].astype(jnp.bfloat16)
            else:
                sums(half, way, step - 1).wait_recv()
                own = 2 * d - 1 + way
                for got, cols in ((0, slice(0, MID)), (1, slice(MID, WIDTH))):
                    x = part[half, own, :, cols]
                    if step > 1 or got == way:
                        x = x + in_buf[half, way, step - 1, :, cols].astype(jnp.float32)
                    out_buf[half, way, step, :, cols] = x.astype(jnp.bfloat16)
            sums(half, way, step).start()

    def finish(half):
        total = part[half, 0] + rows[half, y].astype(jnp.float32)
        for way in range(2):
            sums(half, way, 3).wait_recv()
            total = total + in_buf[half, way, 3].astype(jnp.float32)
        out_ref[half * ROWS : (half + 1) * ROWS, :] = (
            layer_norm(total) * gain_ref[1:2, :]
        ).astype(jnp.bfloat16)

    start = attend(0, 0)
    pl.semaphore_wait(barrier, TOKENS + 1)
    exchange(0)
    attend(1, start)
    exchange(1)
    for half in range(HALVES):
        mix(half)
        for way in range(2):
            gather(half, way, 1).start()
    forward(0, 1)
    forward(1, 1)
    loads[2].wait()
    loads[3].wait()
    forward(0, 2)
    ffn(0, 0, 5)
    forward(1, 2)
    forward(0, 3)
    ffn(1, 0, 5)
    forward(1, 3)
    forward(0, 4)
    ffn(0, 5, 8)
    scatter(0, 0)
    forward(1, 4)
    ffn(1, 5, 8)
    scatter(1, 0)
    for step in range(1, 4):
        scatter(0, step)
        scatter(1, step)
    finish(0)
    finish(1)

    for half in range(HALVES):
        all_tiles(tiles, half, a2a_send).wait()
        for way in range(2):
            for hop in range(1, 5):
                gather(half, way, hop).wait_send()
            for step in range(4):
                sums(half, way, step).wait_send()


def local(hist_len, queries, history_keys, cached_history_values, gain_mix, w_up, w_down, gain_out):
    vmem = pl.BlockSpec(memory_space=pltpu.VMEM)
    hbm = pl.BlockSpec(memory_space=pl.ANY)
    bf16, f32 = jnp.bfloat16, jnp.float32
    dma = pltpu.SemaphoreType.DMA
    out = pl.pallas_call(
        kernel,
        out_shape=jax.ShapeDtypeStruct((REQ_DEV, WIDTH), bf16),
        in_specs=[pl.BlockSpec(memory_space=pltpu.SMEM), vmem, vmem, hbm, hbm, hbm, hbm],
        out_specs=vmem,
        scratch_shapes=[
            pltpu.VMEM((SLOTS, HEAD, POS), bf16),
            pltpu.VMEM((SLOTS, HEAD, POS), bf16),
            pltpu.VMEM(w_up.shape[1:], bf16),
            pltpu.VMEM(w_down.shape[1:], bf16),
            pltpu.VMEM((ROWS * TOKENS, 128), f32),
            pltpu.VMEM((HALVES, TOKENS, ROWS, 128), bf16),
            pltpu.VMEM((HALVES, TOKENS, ROWS, 128), bf16),
            pltpu.VMEM((HALVES, RING, ROWS, WIDTH), bf16),
            pltpu.VMEM((HALVES, RING, ROWS, WIDTH), f32),
            pltpu.VMEM((HALVES, 2, 4, ROWS, WIDTH), bf16),
            pltpu.VMEM((HALVES, 2, 4, ROWS, WIDTH), bf16),
            dma((4,)),
            dma((HALVES,)),
            dma((HALVES,)),
            dma((HALVES, 2, 4)),
            dma((HALVES, 2, 4)),
            dma((HALVES, 2, 4)),
            dma((HALVES, 2, 4)),
        ],
        compiler_params=pltpu.CompilerParams(
            collective_id=0, has_side_effects=True, vmem_limit_bytes=60 * 2**20
        ),
        cost_estimate=pl.CostEstimate(
            flops=700_000_000, bytes_accessed=5_000_000, transcendentals=500_000
        ),
    )(
        hist_len, queries, jnp.stack([gain_mix, gain_out]),
        history_keys, cached_history_values, w_up, w_down,
    )
    return out.reshape(REQ_DEV, 1, WIDTH)


def solution(mesh):
    return jax.shard_map(
        local,
        mesh=mesh,
        in_specs=(
            P(),
            P(None, "token"),
            P(("batch", "hidden"), "token", None),
            P(("batch", "hidden"), "token", None),
            P(),
            P("token", None, "hidden"),
            P("token", "hidden", None),
            P(),
        ),
        out_specs=P(("batch", "hidden"), "token", None),
        check_vma=False,
    )
```

time: 88.8 us -> 58 us (0.65)
  Pallas kernels: 0 us -> 54.2 us
  blocking collectives: 50.1 us -> 0 us
  waiting for transfers between devices: 16.8 us -> 0 us
  matrix products: 9.73 us -> 0 us
  starting transfers between devices: 5.24 us -> 0 us
  other arithmetic: 3.89 us -> 0.61 us
    pallas_call x0 -> x1, Pallas kernels: none -> 54.2 us  [local(): pl.pallas_call(kernel, out_shape=jax.ShapeDtypeStruct((REQ_DEV, WIDTH), b...]
    all_gather x1 -> x0, blocking collectives: 27.8 us -> none  [local(): lax.all_gather(normed, 'hidden', axis=0, tiled=True)]
    all_to_all x1 -> x0, blocking collectives: 22.2 us -> none  [local(): lax.all_to_all(attended.reshape(REQ_DEV, TOKEN_COUNT, local_heads * head_...]
    all_to_all x1 -> x0, waiting for transfers between devices: 16.8 us -> none  [sent_and_summed(): parts = lax.all_to_all(in_blocks(x, dim, length), axis, 0, 0, tiled=True)]
    dot_general x6 -> x0, matrix products: 9.73 us -> none  [the longest x1 4.37 us: local(): jnp.einsum('ntf,tfd->ntd', activated, w_down, preferred_element_type=jnp....]
    all_to_all x1 -> x0, starting transfers between devices: 5.24 us -> none  [sent_and_summed(): parts = lax.all_to_all(in_blocks(x, dim, length), axis, 0, 0, tiled=True)]
    reduce_sum x10 -> x0, other arithmetic: 2.47 us -> none  [the longest x1 0.95 us: block_partials(): totals = jnp.sum(softmax_terms, axis=-1)]
    another operation x0 -> x2, local copies, waits for them, and re-layouts: none -> 1.4 us  [local(): jnp.stack([gain_mix, gain_out])]
  transfers between devices with their start and end apart: 1 -> 0, of which waited for: 1 -> 0; matrix products, arithmetic and copies ran while one was open for 0% -> 0% of each run, Pallas kernels for 0% -> 0%
where the time goes in v1:
time: 58 us; the launch traced here: 57.8 us
  Pallas kernels  54.2 us (93%)
  local copies, waits for them, and re-layouts  2.94 us (5%)
  other arithmetic  0.61 us (1%)
    pallas_call x1, Pallas kernels, local(): pl.pallas_call(kernel, out_shape=jax.ShapeDtypeStruct((REQ_DEV, WIDTH), b...  54.2 us
    unnamed x1, local copies, waits for them, and re-layouts  1.54 us
    another operation x2, local copies, waits for them, and re-layouts, local(): jnp.stack([gain_mix, gain_out])  1.4 us

profile of v1, /device:TPU:2, one launch (start us, length us, event | category | flops | bytes accessed | tf_op | source)
XLA Modules:
  0.0 57.8 jit_solution(9412703798895391011)
XLA Ops:
  0.0 0.7 %stack.9 = f32[1,1536]{1,0:T(1,128)S(1)} reshape(f32[1536]{0:T(1024)} %param.12) | data formatting | bytes 12288 | tf_op jit(solution)/shard_map/stack | solution.py:305
  0.7 0.7 %stack.10 = f32[1,1536]{1,0:T(1,128)S(1)} reshape(f32[1536]{0:T(1024)} %param.15) | data formatting | bytes 12288 | tf_op jit(solution)/shard_map/stack | solution.py:305
  1.4 0.6 %pad_maximum_fusion.gain_ref = f32[2,1536]{1,0:T(2,128)} fusion(f32[1,1536]{1,0:T(1,128)S(1)} %stack.10, f32[1,1536]{1,0:T(1,128)S(1)} %stack.9), kind=kLoop, calls=%fused_computation | loop fusion | flops 3072 | bytes 24576 | tf_op jit(solution)/shard_map/stack | solution.py:305
  2.0 54.2 %shard_map.82 = bf16[32,1536]{1,0:T(8,128)(2,1)} custom-call(s32[512]{0:T(512)} %len_ref.1, bf16[32,48]{1,0:T(8,128)(2,1)} %q_ref.1, f32[2,1536]{1,0:T(2,128)} %pad_maximum_fusion.gain_ref, bf16[96,48,128]{2,1,0:T(8,128)(2,1)} %k_hbm.1, bf16[96,48,128]{2,1,0:T(8,128)(2,1)} %v_hbm.1, bf16[1,1536,384]{2,1,0:T(8,128)(2,1)} %up_hbm.1, bf16[1,384,1536]{2,1,0:T(8,128)(2,1)} %down_hbm.1), custom_call_target="tpu_custom_call" | custom-call | flops 700000000 | bytes 5000000 | tf_op jit(solution)/shard_map/pallas_call | solution.py:273
  56.2 1.5 %copy.10 = bf16[32,1,1536]{2,0,1:T(8,128)(2,1)} copy(bf16[32,1,1536]{2,0,1:T(8,128)(2,1)} %bitcast.1) | data formatting | bytes 196608

commit v2 on v1

v2 whole, which is shorter than its diff:
```python
import functools
import math

import jax
import jax.numpy as jnp
from jax import lax
from jax.experimental import pallas as pl
from jax.experimental.pallas import tpu as pltpu
from jax.sharding import PartitionSpec as P

TOKENS = 32
WIDTH = 1536
HEAD = 48
POS = 128
REQ_DEV = 32
SLOTS = 96
RING = 8
HALVES = 2
ROWS = REQ_DEV // HALVES
PAIR_SLOTS = 6
PAIRS = REQ_DEV // 2
UNROLL = 4
MID = WIDTH // 2
FILL = -1e30
EPSILON = 1e-5
MESH = pl.DeviceIdType.MESH
SIDE = 8
OFFSETS = sorted(
    ((dx, dz) for dx in range(TOKENS // SIDE) for dz in range(SIDE) if dx or dz),
    key=lambda o: (-min(o[0], TOKENS // SIDE - o[0]) - min(o[1], SIDE - o[1]), o),
)


def layer_norm(x):
    mean = jnp.sum(x, axis=-1, keepdims=True) * (1.0 / WIDTH)
    c = x - mean
    var = jnp.sum(c * c, axis=-1, keepdims=True) * (1.0 / WIDTH)
    return c * lax.rsqrt(var + EPSILON)


def kernel(
    len_ref, q_ref, mix_gain, out_gain, k_hbm, v_hbm, up_hbm, down_hbm,
    out_ref,
    k_ref, v_ref, up_ref, down_ref, att, tiles, others, rows, part, out_buf, in_buf,
    load_sem, a2a_send, a2a_recv, ag_send, ag_recv, rs_send, rs_recv,
):
    me = lax.axis_index("token")
    y = lax.axis_index("hidden")
    group = lax.axis_index("batch") * RING + y

    def at(distance):
        return lax.rem(y + RING + distance, RING)


    def peer(offset):
        x, z = me // SIDE, lax.rem(me, SIDE)
        return lax.rem(x + offset[0], TOKENS // SIDE) * SIDE + lax.rem(z + offset[1], SIDE)

    barrier = pltpu.get_barrier_semaphore()
    for offset in OFFSETS:
        pl.semaphore_signal(
            barrier, inc=1, device_id={"token": peer(offset)}, device_id_type=MESH
        )
    for step in (2, -2, 1, -1):
        pl.semaphore_signal(
            barrier, inc=1, device_id={"hidden": at(step)}, device_id_type=MESH
        )

    loads = [
        pltpu.make_async_copy(k_hbm, k_ref, load_sem.at[0]),
        pltpu.make_async_copy(v_hbm, v_ref, load_sem.at[1]),
        pltpu.make_async_copy(up_hbm.at[0], up_ref, load_sem.at[2]),
        pltpu.make_async_copy(down_hbm.at[0], down_ref, load_sem.at[3]),
    ]
    for load in loads:
        load.start()

    att[...] = jnp.zeros_like(att)
    position = lax.broadcasted_iota(jnp.int32, (1, PAIR_SLOTS * POS), 1)
    scale = HEAD ** -0.5
    lane = lax.broadcasted_iota(jnp.int32, (ROWS, 128), 1)
    loads[0].wait()
    loads[1].wait()

    def attend_pair(pair, start):
        request = group * REQ_DEV + pair * 2
        len_a, len_b = len_ref[request], len_ref[request + 1]
        used_a = lax.shift_right_logical(len_a + (POS - 1), 7)
        used_b = lax.shift_right_logical(len_b + (POS - 1), 7)
        slot = [jnp.minimum(start + i, SLOTS - 1) for i in range(PAIR_SLOTS)]
        keys = jnp.concatenate([k_ref[s] for s in slot], axis=1)
        values = jnp.concatenate([v_ref[s] for s in slot], axis=1)
        score = jnp.dot(q_ref[...], keys, preferred_element_type=jnp.float32) * scale
        edge = used_a * POS
        of_a = position < edge
        in_a = position < len_a
        in_b = jnp.logical_and(position >= edge, position < edge + len_b)
        max_a = jnp.max(jnp.where(in_a, score, FILL), axis=1, keepdims=True)
        max_b = jnp.max(jnp.where(in_b, score, FILL), axis=1, keepdims=True)
        term = jnp.exp(score - jnp.where(of_a, max_a, max_b))
        term_a = jnp.where(in_a, term, 0.0)
        term_b = jnp.where(in_b, term, 0.0)
        both = jnp.concatenate([term_a, term_b], axis=0)
        total = jnp.sum(both, axis=1, keepdims=True)
        acc = lax.dot_general(
            both.astype(jnp.bfloat16), values, (((1,), (1,)), ((), ())),
            preferred_element_type=jnp.float32,
        )
        row = pl.multiple_of(pair * (2 * TOKENS), 2 * TOKENS)
        att[pl.ds(row, 2 * TOKENS), 0:HEAD] = acc / total
        return start + used_a + used_b

    def attend():
        def step(i, start):
            for u in range(UNROLL):
                start = attend_pair(i * UNROLL + u, start)
            return start

        lax.fori_loop(0, PAIRS // UNROLL, step, 0)
        for q in range(TOKENS):
            first = att[pl.ds(q, ROWS, stride=TOKENS), :]
            second = att[pl.ds(ROWS * TOKENS + q, ROWS, stride=TOKENS), :]
            tile = jnp.where(lane < 64, first, pltpu.roll(second, 64, 1))
            tiles[q] = tile.astype(jnp.bfloat16)
        others[me] = tiles[me]

    def exchange():
        for offset in OFFSETS:
            to = peer(offset)
            pltpu.make_async_remote_copy(
                src_ref=tiles.at[to],
                dst_ref=others.at[me],
                send_sem=a2a_send,
                recv_sem=a2a_recv,
                device_id={"token": to},
                device_id_type=MESH,
            ).start()

    def all_tiles(ref, sem):
        some = ref.at[pl.ds(0, TOKENS - 1)]
        return pltpu.make_async_copy(some, some, sem)

    def mix(half):
        out = [None] * (WIDTH // 128)
        for j in range(TOKENS):
            x = tiles[j].astype(jnp.float32) + others[j].astype(jnp.float32)
            first = j * HEAD
            shift = first % 128
            turn = (shift + 64 * half) % 128
            if turn:
                x = pltpu.roll(x, turn, 1)
            t = first // 128
            if shift + HEAD > 128:
                out[t] = jnp.where(lane >= shift, x, out[t])
                out[t + 1] = x
            else:
                out[t] = x if out[t] is None else jnp.where(lane >= shift, x, out[t])
        normed = layer_norm(jnp.concatenate(out, axis=1)) * mix_gain[...].reshape(1, WIDTH)
        rows[half, y] = normed.astype(jnp.bfloat16)

    cols = (pl.ds(0, MID), pl.ds(MID, MID))
    sides = (slice(0, MID), slice(MID, WIDTH))

    def gather(half, way, kind, mine):
        sign = 1 - 2 * way
        reach = 1 + kind % 2
        source = (0, 0, -2, -2)[kind] if mine else (-1, -2, -3, -4)[kind]
        block = rows.at[half, at(sign * source)]
        if kind == 3:
            block = block.at[:, cols[way]]
        return pltpu.make_async_remote_copy(
            src_ref=block, dst_ref=block,
            send_sem=ag_send.at[half, way, kind], recv_sem=ag_recv.at[half, way, kind],
            device_id={"hidden": at(sign * reach)}, device_id_type=MESH,
        )

    def begin(half):
        for kind in (1, 0):
            for way in range(2):
                gather(half, way, kind, True).start()

    def forward(half):
        for way in range(2):
            gather(half, way, 1, False).wait_recv()
            for kind in (3, 2):
                gather(half, way, kind, True).start()

    def near(half):
        for way in range(2):
            gather(half, way, 0, False).wait_recv()

    def far(half):
        for kind in (2, 3):
            for way in range(2):
                gather(half, way, kind, False).wait_recv()

    ORDER = [0, -1, 1, -2, 2, -3, 3, 4]

    def ffn(half, first, last):
        x = jnp.concatenate(
            [rows[half, at(ORDER[i])] for i in range(first, last)], axis=0
        )
        up = jnp.dot(x, up_ref[...], preferred_element_type=jnp.float32)
        act = (0.5 * up * (1.0 + lax.erf(up * math.sqrt(0.5)))).astype(jnp.bfloat16)
        down = jnp.dot(act, down_ref[...], preferred_element_type=jnp.float32)
        part[half, first:last] = down.reshape(last - first, ROWS, WIDTH)

    def sums(half, way, kind):
        sign = 2 * way - 1
        src, dst = out_buf.at[half, way, kind], in_buf.at[half, way, kind]
        if kind == 2:
            src, dst = src.at[:, cols[way]], dst.at[:, cols[way]]
        return pltpu.make_async_remote_copy(
            src_ref=src, dst_ref=dst,
            send_sem=rs_send.at[half, way, kind], recv_sem=rs_recv.at[half, way, kind],
            device_id={"hidden": at(sign * (1, 1, 2, 2)[kind])}, device_id_type=MESH,
        )

    def scatter(half, kind):
        for way in range(2):
            if kind == 2:
                out_buf[half, way, 2, :, sides[way]] = part[half, 7, :, sides[way]].astype(jnp.bfloat16)
            elif kind == 3:
                sums(half, way, 2).wait_recv()
                sums(half, way, 1).wait_recv()
                for side in range(2):
                    c = sides[side]
                    x = part[half, 3 + way, :, c] + in_buf[half, way, 1, :, c].astype(jnp.float32)
                    if side == way:
                        x = x + in_buf[half, way, 2, :, c].astype(jnp.float32)
                    out_buf[half, way, 3, :, c] = x.astype(jnp.bfloat16)
            else:
                out_buf[half, way, kind] = part[half, (1, 5)[kind] + way].astype(jnp.bfloat16)
            sums(half, way, kind).start()

    def finish(half):
        total = part[half, 0] + rows[half, y].astype(jnp.float32)
        for kind in (0, 3):
            for way in range(2):
                sums(half, way, kind).wait_recv()
                total = total + in_buf[half, way, kind].astype(jnp.float32)
        out_ref[half * ROWS : (half + 1) * ROWS, :] = (
            layer_norm(total) * out_gain[...].reshape(1, WIDTH)
        ).astype(jnp.bfloat16)

    attend()
    pl.semaphore_wait(barrier, len(OFFSETS) + 4)
    exchange()
    all_tiles(others, a2a_recv).wait()
    for half in range(HALVES):
        mix(half)
        begin(half)
    loads[2].wait()
    loads[3].wait()
    forward(0)
    near(0)
    ffn(0, 0, 5)
    forward(1)
    scatter(0, 0)
    near(1)
    ffn(1, 0, 5)
    far(0)
    ffn(0, 5, 8)
    scatter(0, 2)
    scatter(0, 1)
    scatter(1, 0)
    far(1)
    ffn(1, 5, 8)
    scatter(1, 2)
    scatter(1, 1)
    scatter(0, 3)
    scatter(1, 3)
    finish(0)
    finish(1)

    all_tiles(tiles, a2a_send).wait()
    for half in range(HALVES):
        for way in range(2):
            for kind in range(4):
                gather(half, way, kind, True).wait_send()
                sums(half, way, kind).wait_send()


def local(hist_len, queries, history_keys, cached_history_values, gain_mix, w_up, w_down, gain_out):
    vmem = pl.BlockSpec(memory_space=pltpu.VMEM)
    hbm = pl.BlockSpec(memory_space=pl.ANY)
    bf16, f32 = jnp.bfloat16, jnp.float32
    dma = pltpu.SemaphoreType.DMA
    out = pl.pallas_call(
        kernel,
        out_shape=jax.ShapeDtypeStruct((REQ_DEV, WIDTH), bf16),
        in_specs=[pl.BlockSpec(memory_space=pltpu.SMEM), vmem, vmem, vmem, hbm, hbm, hbm, hbm],
        out_specs=vmem,
        scratch_shapes=[
            pltpu.VMEM((SLOTS, HEAD, POS), bf16),
            pltpu.VMEM((SLOTS, HEAD, POS), bf16),
            pltpu.VMEM(w_up.shape[1:], bf16),
            pltpu.VMEM(w_down.shape[1:], bf16),
            pltpu.VMEM((REQ_DEV * TOKENS, 128), f32),
            pltpu.VMEM((TOKENS, ROWS, 128), bf16),
            pltpu.VMEM((TOKENS, ROWS, 128), bf16),
            pltpu.VMEM((HALVES, RING, ROWS, WIDTH), bf16),
            pltpu.VMEM((HALVES, RING, ROWS, WIDTH), f32),
            pltpu.VMEM((HALVES, 2, 4, ROWS, WIDTH), bf16),
            pltpu.VMEM((HALVES, 2, 4, ROWS, WIDTH), bf16),
            dma((4,)),
            dma(()),
            dma(()),
            dma((HALVES, 2, 4)),
            dma((HALVES, 2, 4)),
            dma((HALVES, 2, 4)),
            dma((HALVES, 2, 4)),
        ],
        compiler_params=pltpu.CompilerParams(
            collective_id=0, has_side_effects=True, vmem_limit_bytes=60 * 2**20
        ),
        cost_estimate=pl.CostEstimate(
            flops=700_000_000, bytes_accessed=5_000_000, transcendentals=500_000
        ),
    )(
        hist_len, queries, gain_mix, gain_out,
        history_keys, cached_history_values, w_up, w_down,
    )
    return out.reshape(REQ_DEV, 1, WIDTH)


def solution(mesh):
    return jax.shard_map(
        local,
        mesh=mesh,
        in_specs=(
            P(),
            P(None, "token"),
            P(("batch", "hidden"), "token", None),
            P(("batch", "hidden"), "token", None),
            P(),
            P("token", None, "hidden"),
            P("token", "hidden", None),
            P(),
        ),
        out_specs=P(("batch", "hidden"), "token", None),
        check_vma=False,
    )
```

time: 58 us -> 51.5 us (0.89)
  the two profiles are of different devices: /device:TPU:2 before, /device:TPU:16 now
where the time goes in v2:
time: 51.5 us; the launch traced here: 51.3 us
  Pallas kernels  49.8 us (97%)
  local copies, waits for them, and re-layouts  1.54 us (3%)
    pallas_call x1, Pallas kernels, local(): pl.pallas_call(kernel, out_shape=jax.ShapeDtypeStruct((REQ_DEV, WIDTH), b...  49.8 us
    unnamed x1, local copies, waits for them, and re-layouts  1.54 us

profile of v2, /device:TPU:16, one launch (start us, length us, event | category | flops | bytes accessed | tf_op | source)
XLA Modules:
  0.0 51.3 jit_solution(11322977420816008790)
XLA Ops:
  0.0 49.8 %shard_map.82 = bf16[32,1536]{1,0:T(8,128)(2,1)} custom-call(s32[512]{0:T(512)} %len_ref.1, bf16[32,48]{1,0:T(8,128)(2,1)} %q_ref.1, f32[1536]{0:T(1024)} %mix_gain.1, f32[1536]{0:T(1024)} %out_gain.1, bf16[96,48,128]{2,1,0:T(8,128)(2,1)} %k_hbm.1, bf16[96,48,128]{2,1,0:T(8,128)(2,1)} %v_hbm.1, bf16[1,1536,384]{2,1,0:T(8,128)(2,1)} %up_hbm.1, ...), custom_call_target="tpu_custom_call" | custom-call | flops 700000000 | bytes 5000000 | tf_op jit(solution)/shard_map/pallas_call | solution.py:289
  49.8 1.5 %copy.10 = bf16[32,1,1536]{2,0,1:T(8,128)(2,1)} copy(bf16[32,1,1536]{2,0,1:T(8,128)(2,1)} %bitcast.1) | data formatting | bytes 196608

commit v3 on v2

--- a/solution.py
+++ b/solution.py
@@ -19,8 +19,9 @@
 ROWS = REQ_DEV // HALVES
 PAIR_SLOTS = 6
 PAIRS = REQ_DEV // 2
-UNROLL = 4
+GROUP = 16
 MID = WIDTH // 2
+KEEP = (0, 1, 1, 2, 3, 3)
 FILL = -1e30
 EPSILON = 1e-5
 MESH = pl.DeviceIdType.MESH
@@ -39,9 +40,9 @@
 
 
 def kernel(
-    len_ref, q_ref, mix_gain, out_gain, k_hbm, v_hbm, up_hbm, down_hbm,
+    len_hbm, q_hbm, mix_hbm, gain_hbm, k_hbm, v_hbm, up_hbm, down_hbm,
     out_ref,
-    k_ref, v_ref, up_ref, down_ref, att, tiles, others, rows, part, out_buf, in_buf,
+    len_ref, q_ref, mix_gain, out_gain, k_ref, v_ref, up_ref, down_ref, att, tiles, others, rows, part, out_buf, in_buf,
     load_sem, a2a_send, a2a_recv, ag_send, ag_recv, rs_send, rs_recv,
 ):
     me = lax.axis_index("token")
@@ -71,52 +72,64 @@
         pltpu.make_async_copy(v_hbm, v_ref, load_sem.at[1]),
         pltpu.make_async_copy(up_hbm.at[0], up_ref, load_sem.at[2]),
         pltpu.make_async_copy(down_hbm.at[0], down_ref, load_sem.at[3]),
+        pltpu.make_async_copy(len_hbm, len_ref, load_sem.at[4]),
+        pltpu.make_async_copy(q_hbm, q_ref, load_sem.at[5]),
+        pltpu.make_async_copy(mix_hbm, mix_gain, load_sem.at[6]),
+        pltpu.make_async_copy(gain_hbm, out_gain, load_sem.at[7]),
     ]
-    for load in loads:
-        load.start()
+    for i in (4, 5, 0, 1, 6, 7):
+        loads[i].start()
 
     att[...] = jnp.zeros_like(att)
     position = lax.broadcasted_iota(jnp.int32, (1, PAIR_SLOTS * POS), 1)
     scale = HEAD ** -0.5
     lane = lax.broadcasted_iota(jnp.int32, (ROWS, 128), 1)
-    loads[0].wait()
-    loads[1].wait()
-
-    def attend_pair(pair, start):
-        request = group * REQ_DEV + pair * 2
-        len_a, len_b = len_ref[request], len_ref[request + 1]
-        used_a = lax.shift_right_logical(len_a + (POS - 1), 7)
-        used_b = lax.shift_right_logical(len_b + (POS - 1), 7)
-        slot = [jnp.minimum(start + i, SLOTS - 1) for i in range(PAIR_SLOTS)]
-        keys = jnp.concatenate([k_ref[s] for s in slot], axis=1)
-        values = jnp.concatenate([v_ref[s] for s in slot], axis=1)
-        score = jnp.dot(q_ref[...], keys, preferred_element_type=jnp.float32) * scale
-        edge = used_a * POS
-        of_a = position < edge
-        in_a = position < len_a
-        in_b = jnp.logical_and(position >= edge, position < edge + len_b)
-        max_a = jnp.max(jnp.where(in_a, score, FILL), axis=1, keepdims=True)
-        max_b = jnp.max(jnp.where(in_b, score, FILL), axis=1, keepdims=True)
-        term = jnp.exp(score - jnp.where(of_a, max_a, max_b))
-        term_a = jnp.where(in_a, term, 0.0)
-        term_b = jnp.where(in_b, term, 0.0)
-        both = jnp.concatenate([term_a, term_b], axis=0)
-        total = jnp.sum(both, axis=1, keepdims=True)
-        acc = lax.dot_general(
-            both.astype(jnp.bfloat16), values, (((1,), (1,)), ((), ())),
-            preferred_element_type=jnp.float32,
-        )
-        row = pl.multiple_of(pair * (2 * TOKENS), 2 * TOKENS)
-        att[pl.ds(row, 2 * TOKENS), 0:HEAD] = acc / total
-        return start + used_a + used_b
+    for i in (4, 5, 0):
+        loads[i].wait()
+    loads[2].start()
+    loads[3].start()
+
+    def attend_group(first, start):
+        lens, uses, slots, scores, terms, totals = [], [], [], [], [], []
+        for i in range(GROUP):
+            request = group * REQ_DEV + (first + i) * 2
+            len_a, len_b = len_ref[request], len_ref[request + 1]
+            used_a = lax.shift_right_logical(len_a + (POS - 1), 7)
+            used_b = lax.shift_right_logical(len_b + (POS - 1), 7)
+            lens.append((len_a, len_b))
+            uses.append(used_a * POS)
+            slots.append([jnp.minimum(start + i, SLOTS - 1) for i in range(PAIR_SLOTS)])
+            start = start + used_a + used_b
+        for i in range(GROUP):
+            keys = jnp.concatenate([k_ref[s] for s in slots[i]], axis=1)
+            scores.append(jnp.dot(q_ref[...], keys, preferred_element_type=jnp.float32) * scale)
+        for i in range(GROUP):
+            (len_a, len_b), edge = lens[i], uses[i]
+            in_a = position < len_a
+            in_b = jnp.logical_and(position >= edge, position < edge + len_b)
+            max_a = jnp.max(jnp.where(in_a, scores[i], FILL), axis=1, keepdims=True)
+            max_b = jnp.max(jnp.where(in_b, scores[i], FILL), axis=1, keepdims=True)
+            term = jnp.exp(scores[i] - jnp.where(position < edge, max_a, max_b))
+            both = jnp.concatenate(
+                [jnp.where(in_a, term, 0.0), jnp.where(in_b, term, 0.0)], axis=0
+            )
+            totals.append(jnp.sum(both, axis=1, keepdims=True))
+            terms.append(both.astype(jnp.bfloat16))
+        if first == 0:
+            loads[1].wait()
+        for i in range(GROUP):
+            values = jnp.concatenate([v_ref[s] for s in slots[i]], axis=1)
+            acc = lax.dot_general(
+                terms[i], values, (((1,), (1,)), ((), ())), preferred_element_type=jnp.float32
+            )
+            row = (first + i) * 2 * TOKENS
+            att[row : row + 2 * TOKENS, 0:HEAD] = acc / totals[i]
+        return start
 
     def attend():
-        def step(i, start):
-            for u in range(UNROLL):
-                start = attend_pair(i * UNROLL + u, start)
-            return start
-
-        lax.fori_loop(0, PAIRS // UNROLL, step, 0)
+        start = 0
+        for first in range(0, PAIRS, GROUP):
+            start = attend_group(first, start)
         for q in range(TOKENS):
             first = att[pl.ds(q, ROWS, stride=TOKENS), :]
             second = att[pl.ds(ROWS * TOKENS + q, ROWS, stride=TOKENS), :]
@@ -163,11 +176,11 @@
 
     def gather(half, way, kind, mine):
         sign = 1 - 2 * way
-        reach = 1 + kind % 2
-        source = (0, 0, -2, -2)[kind] if mine else (-1, -2, -3, -4)[kind]
+        reach = (1, 2, 2, 1, 1, 2)[kind]
+        source = (0, 0, 0, -2, -2, -2)[kind] - (0 if mine else reach)
         block = rows.at[half, at(sign * source)]
-        if kind == 3:
-            block = block.at[:, cols[way]]
+        if kind:
+            block = block.at[:, cols[(0, 1, 0, 1, way)[kind - 1]]]
         return pltpu.make_async_remote_copy(
             src_ref=block, dst_ref=block,
             send_sem=ag_send.at[half, way, kind], recv_sem=ag_recv.at[half, way, kind],
@@ -175,22 +188,29 @@
         )
 
     def begin(half):
-        for kind in (1, 0):
+        for turn in range(2):
             for way in range(2):
-                gather(half, way, kind, True).start()
+                gather(half, way, 1 + (way ^ turn), True).start()
+
+    def begin_near(half):
+        for way in range(2):
+            gather(half, way, 0, True).start()
 
     def forward(half):
-        for way in range(2):
-            gather(half, way, 1, False).wait_recv()
-            for kind in (3, 2):
-                gather(half, way, kind, True).start()
+        for turn in range(2):
+            for way in range(2):
+                side = way ^ turn
+                gather(half, way, 1 + side, False).wait_recv()
+                if turn == 0:
+                    gather(half, way, 5, True).start()
+                gather(half, way, 3 + side, True).start()
 
     def near(half):
         for way in range(2):
             gather(half, way, 0, False).wait_recv()
 
     def far(half):
-        for kind in (2, 3):
+        for kind in (5, 3, 4):
             for way in range(2):
                 gather(half, way, kind, False).wait_recv()
 
@@ -207,38 +227,56 @@
 
     def sums(half, way, kind):
         sign = 2 * way - 1
-        src, dst = out_buf.at[half, way, kind], in_buf.at[half, way, kind]
-        if kind == 2:
-            src, dst = src.at[:, cols[way]], dst.at[:, cols[way]]
+        src, dst = out_buf.at[half, way, KEEP[kind]], in_buf.at[half, way, KEEP[kind]]
+        if kind:
+            c = cols[(0, 1, way, 0, 1)[kind - 1]]
+            src, dst = src.at[:, c], dst.at[:, c]
         return pltpu.make_async_remote_copy(
             src_ref=src, dst_ref=dst,
             send_sem=rs_send.at[half, way, kind], recv_sem=rs_recv.at[half, way, kind],
-            device_id={"hidden": at(sign * (1, 1, 2, 2)[kind])}, device_id_type=MESH,
-        )
-
-    def scatter(half, kind):
-        for way in range(2):
-            if kind == 2:
-                out_buf[half, way, 2, :, sides[way]] = part[half, 7, :, sides[way]].astype(jnp.bfloat16)
-            elif kind == 3:
-                sums(half, way, 2).wait_recv()
-                sums(half, way, 1).wait_recv()
-                for side in range(2):
-                    c = sides[side]
-                    x = part[half, 3 + way, :, c] + in_buf[half, way, 1, :, c].astype(jnp.float32)
-                    if side == way:
-                        x = x + in_buf[half, way, 2, :, c].astype(jnp.float32)
-                    out_buf[half, way, 3, :, c] = x.astype(jnp.bfloat16)
-            else:
-                out_buf[half, way, kind] = part[half, (1, 5)[kind] + way].astype(jnp.bfloat16)
-            sums(half, way, kind).start()
+            device_id={"hidden": at(sign * (1, 1, 1, 2, 2, 2)[kind])}, device_id_type=MESH,
+        )
+
+    def put(half, way, kind, c, x):
+        out_buf[half, way, KEEP[kind], :, c] = x.astype(jnp.bfloat16)
+        sums(half, way, kind).start()
+
+    def scatter_near(half):
+        for way in range(2):
+            put(half, way, 0, slice(0, WIDTH), part[half, 1 + way])
+
+    def scatter(half):
+        for way in range(2):
+            c = sides[1 - way]
+            put(half, way, 2 - way, c, part[half, 5 + way, :, c])
+        for way in range(2):
+            c = sides[way]
+            put(half, way, 3, c, part[half, 7, :, c])
+        for way in range(2):
+            c = sides[way]
+            put(half, way, 1 + way, c, part[half, 5 + way, :, c])
+
+    def relay(half):
+        for turn in range(2):
+            for way in range(2):
+                side = 1 - way if turn == 0 else way
+                c = sides[side]
+                sums(half, way, 1 + side).wait_recv()
+                x = part[half, 3 + way, :, c] + in_buf[half, way, 1, :, c].astype(jnp.float32)
+                if turn:
+                    sums(half, way, 3).wait_recv()
+                    x = x + in_buf[half, way, 2, :, c].astype(jnp.float32)
+                put(half, way, 4 + side, c, x)
 
     def finish(half):
         total = part[half, 0] + rows[half, y].astype(jnp.float32)
-        for kind in (0, 3):
-            for way in range(2):
-                sums(half, way, kind).wait_recv()
-                total = total + in_buf[half, way, kind].astype(jnp.float32)
+        for way in range(2):
+            sums(half, way, 0).wait_recv()
+            total = total + in_buf[half, way, 0].astype(jnp.float32)
+        for way in range(2):
+            sums(half, way, 4).wait_recv()
+            sums(half, way, 5).wait_recv()
+            total = total + in_buf[half, way, 3].astype(jnp.float32)
         out_ref[half * ROWS : (half + 1) * ROWS, :] = (
             layer_norm(total) * out_gain[...].reshape(1, WIDTH)
         ).astype(jnp.bfloat16)
@@ -247,36 +285,38 @@
     pl.semaphore_wait(barrier, len(OFFSETS) + 4)
     exchange()
     all_tiles(others, a2a_recv).wait()
+    loads[6].wait()
+    loads[7].wait()
     for half in range(HALVES):
         mix(half)
         begin(half)
+    begin_near(0)
+    begin_near(1)
     loads[2].wait()
     loads[3].wait()
     forward(0)
+    forward(1)
     near(0)
     ffn(0, 0, 5)
-    forward(1)
-    scatter(0, 0)
+    scatter_near(0)
     near(1)
     ffn(1, 0, 5)
     far(0)
     ffn(0, 5, 8)
-    scatter(0, 2)
-    scatter(0, 1)
-    scatter(1, 0)
+    scatter(0)
     far(1)
     ffn(1, 5, 8)
-    scatter(1, 2)
-    scatter(1, 1)
-    scatter(0, 3)
-    scatter(1, 3)
+    scatter(1)
+    scatter_near(1)
+    relay(0)
+    relay(1)
     finish(0)
     finish(1)
 
     all_tiles(tiles, a2a_send).wait()
     for half in range(HALVES):
         for way in range(2):
-            for kind in range(4):
+            for kind in range(6):
                 gather(half, way, kind, True).wait_send()
                 sums(half, way, kind).wait_send()
 
@@ -288,10 +328,14 @@
     dma = pltpu.SemaphoreType.DMA
     out = pl.pallas_call(
         kernel,
-        out_shape=jax.ShapeDtypeStruct((REQ_DEV, WIDTH), bf16),
-        in_specs=[pl.BlockSpec(memory_space=pltpu.SMEM), vmem, vmem, vmem, hbm, hbm, hbm, hbm],
+        out_shape=pltpu.VMEM((REQ_DEV, WIDTH), bf16),
+        in_specs=[hbm] * 8,
         out_specs=vmem,
         scratch_shapes=[
+            pltpu.SMEM(hist_len.shape, hist_len.dtype),
+            pltpu.VMEM(queries.shape, bf16),
+            pltpu.VMEM(gain_mix.shape, f32),
+            pltpu.VMEM(gain_out.shape, f32),
             pltpu.VMEM((SLOTS, HEAD, POS), bf16),
             pltpu.VMEM((SLOTS, HEAD, POS), bf16),
             pltpu.VMEM(w_up.shape[1:], bf16),
@@ -303,13 +347,13 @@
             pltpu.VMEM((HALVES, RING, ROWS, WIDTH), f32),
             pltpu.VMEM((HALVES, 2, 4, ROWS, WIDTH), bf16),
             pltpu.VMEM((HALVES, 2, 4, ROWS, WIDTH), bf16),
-            dma((4,)),
+            dma((8,)),
             dma(()),
             dma(()),
-            dma((HALVES, 2, 4)),
-            dma((HALVES, 2, 4)),
-            dma((HALVES, 2, 4)),
-            dma((HALVES, 2, 4)),
+            dma((HALVES, 2, 6)),
+            dma((HALVES, 2, 6)),
+            dma((HALVES, 2, 6)),
+            dma((HALVES, 2, 6)),
         ],
         compiler_params=pltpu.CompilerParams(
             collective_id=0, has_side_effects=True, vmem_limit_bytes=60 * 2**20

time: 51.5 us -> 46.5 us (0.903)
  the two profiles are of different devices: /device:TPU:16 before, /device:TPU:4 now
where the time goes in v3:
time: 46.5 us; the launch traced here: 46.3 us
  Pallas kernels  45.7 us (98%)
  local copies, waits for them, and re-layouts  0.64 us (1%)
    pallas_call x1, Pallas kernels, local(): pl.pallas_call(kernel, out_shape=pltpu.VMEM((REQ_DEV, WIDTH), bf16), in_s...  45.7 us

profile of v3, /device:TPU:4, one launch (start us, length us, event | category | flops | bytes accessed | tf_op | source)
XLA Modules:
  0.0 46.3 jit_solution(8355048769453753936)
XLA Ops:
  0.0 45.7 %shard_map.82 = bf16[32,1536]{1,0:T(8,128)(2,1)S(1)} custom-call(s32[512]{0:T(512)} %len_hbm.1, bf16[32,48]{1,0:T(8,128)(2,1)} %q_hbm.1, f32[1536]{0:T(1024)} %mix_hbm.1, f32[1536]{0:T(1024)} %gain_hbm.1, bf16[96,48,128]{2,1,0:T(8,128)(2,1)} %k_hbm.1, bf16[96,48,128]{2,1,0:T(8,128)(2,1)} %v_hbm.1, bf16[1,1536,384]{2,1,0:T(8,128)(2,1)} %up_hbm.1, ...), custom_call_target="tpu_custom_call" | custom-call | flops 700000000 | bytes 5000000 | tf_op jit(solution)/shard_map/pallas_call | solution.py:329
  45.7 0.6 %copy.10 = bf16[32,1,1536]{2,0,1:T(8,128)(2,1)} copy(bf16[32,1,1536]{2,0,1:T(8,128)(2,1)S(1)} %bitcast.1) | data formatting | bytes 196608

commit v4 on v3

--- a/solution.py
+++ b/solution.py
@@ -19,7 +19,7 @@
 ROWS = REQ_DEV // HALVES
 PAIR_SLOTS = 6
 PAIRS = REQ_DEV // 2
-GROUP = 16
+GROUP = 8
 MID = WIDTH // 2
 KEEP = (0, 1, 1, 2, 3, 3)
 FILL = -1e30
@@ -126,42 +126,39 @@
             att[row : row + 2 * TOKENS, 0:HEAD] = acc / totals[i]
         return start
 
-    def attend():
-        start = 0
-        for first in range(0, PAIRS, GROUP):
+    def attend(half, start):
+        for first in range(half * PAIRS // HALVES, (half + 1) * PAIRS // HALVES, GROUP):
             start = attend_group(first, start)
         for q in range(TOKENS):
-            first = att[pl.ds(q, ROWS, stride=TOKENS), :]
-            second = att[pl.ds(ROWS * TOKENS + q, ROWS, stride=TOKENS), :]
-            tile = jnp.where(lane < 64, first, pltpu.roll(second, 64, 1))
-            tiles[q] = tile.astype(jnp.bfloat16)
-        others[me] = tiles[me]
-
-    def exchange():
+            tile = att[pl.ds(half * ROWS * TOKENS + q, ROWS, stride=TOKENS), :]
+            tiles[half, q] = tile.astype(jnp.bfloat16)
+        others[half, me] = tiles[half, me]
+        return start
+
+    def exchange(half):
         for offset in OFFSETS:
             to = peer(offset)
             pltpu.make_async_remote_copy(
-                src_ref=tiles.at[to],
-                dst_ref=others.at[me],
-                send_sem=a2a_send,
-                recv_sem=a2a_recv,
+                src_ref=tiles.at[half, to],
+                dst_ref=others.at[half, me],
+                send_sem=a2a_send.at[half],
+                recv_sem=a2a_recv.at[half],
                 device_id={"token": to},
                 device_id_type=MESH,
             ).start()
 
-    def all_tiles(ref, sem):
-        some = ref.at[pl.ds(0, TOKENS - 1)]
-        return pltpu.make_async_copy(some, some, sem)
+    def all_tiles(ref, half, sem):
+        some = ref.at[half, pl.ds(0, TOKENS - 1)]
+        return pltpu.make_async_copy(some, some, sem.at[half])
 
     def mix(half):
         out = [None] * (WIDTH // 128)
         for j in range(TOKENS):
-            x = tiles[j].astype(jnp.float32) + others[j].astype(jnp.float32)
+            x = tiles[half, j].astype(jnp.float32) + others[half, j].astype(jnp.float32)
             first = j * HEAD
             shift = first % 128
-            turn = (shift + 64 * half) % 128
-            if turn:
-                x = pltpu.roll(x, turn, 1)
+            if shift:
+                x = pltpu.roll(x, shift, 1)
             t = first // 128
             if shift + HEAD > 128:
                 out[t] = jnp.where(lane >= shift, x, out[t])
@@ -281,17 +278,18 @@
             layer_norm(total) * out_gain[...].reshape(1, WIDTH)
         ).astype(jnp.bfloat16)
 
-    attend()
+    start = attend(0, 0)
     pl.semaphore_wait(barrier, len(OFFSETS) + 4)
-    exchange()
-    all_tiles(others, a2a_recv).wait()
+    exchange(0)
+    attend(1, start)
+    exchange(1)
     loads[6].wait()
     loads[7].wait()
     for half in range(HALVES):
+        all_tiles(others, half, a2a_recv).wait()
         mix(half)
         begin(half)
-    begin_near(0)
-    begin_near(1)
+        begin_near(half)
     loads[2].wait()
     loads[3].wait()
     forward(0)
@@ -313,8 +311,8 @@
     finish(0)
     finish(1)
 
-    all_tiles(tiles, a2a_send).wait()
     for half in range(HALVES):
+        all_tiles(tiles, half, a2a_send).wait()
         for way in range(2):
             for kind in range(6):
                 gather(half, way, kind, True).wait_send()
@@ -341,15 +339,15 @@
             pltpu.VMEM(w_up.shape[1:], bf16),
             pltpu.VMEM(w_down.shape[1:], bf16),
             pltpu.VMEM((REQ_DEV * TOKENS, 128), f32),
-            pltpu.VMEM((TOKENS, ROWS, 128), bf16),
-            pltpu.VMEM((TOKENS, ROWS, 128), bf16),
+            pltpu.VMEM((HALVES, TOKENS, ROWS, 128), bf16),
+            pltpu.VMEM((HALVES, TOKENS, ROWS, 128), bf16),
             pltpu.VMEM((HALVES, RING, ROWS, WIDTH), bf16),
             pltpu.VMEM((HALVES, RING, ROWS, WIDTH), f32),
             pltpu.VMEM((HALVES, 2, 4, ROWS, WIDTH), bf16),
             pltpu.VMEM((HALVES, 2, 4, ROWS, WIDTH), bf16),
             dma((8,)),
-            dma(()),
-            dma(()),
+            dma((HALVES,)),
+            dma((HALVES,)),
             dma((HALVES, 2, 6)),
             dma((HALVES, 2, 6)),
             dma((HALVES, 2, 6)),

time: 46.5 us -> 46 us (0.989)
  the two profiles are of different devices: /device:TPU:4 before, /device:TPU:16 now
where the time goes in v4:
time: 46 us; the launch traced here: 45.9 us
  Pallas kernels  45.3 us (98%)
  local copies, waits for them, and re-layouts  0.64 us (1%)
    pallas_call x1, Pallas kernels, local(): pl.pallas_call(kernel, out_shape=pltpu.VMEM((REQ_DEV, WIDTH), bf16), in_s...  45.3 us

profile of v4, /device:TPU:16, one launch (start us, length us, event | category | flops | bytes accessed | tf_op | source)
XLA Modules:
  0.0 45.9 jit_solution(3789278595194000479)
XLA Ops:
  0.0 45.3 %shard_map.82 = bf16[32,1536]{1,0:T(8,128)(2,1)S(1)} custom-call(s32[512]{0:T(512)} %len_hbm.1, bf16[32,48]{1,0:T(8,128)(2,1)} %q_hbm.1, f32[1536]{0:T(1024)} %mix_hbm.1, f32[1536]{0:T(1024)} %gain_hbm.1, bf16[96,48,128]{2,1,0:T(8,128)(2,1)} %k_hbm.1, bf16[96,48,128]{2,1,0:T(8,128)(2,1)} %v_hbm.1, bf16[1,1536,384]{2,1,0:T(8,128)(2,1)} %up_hbm.1, ...), custom_call_target="tpu_custom_call" | custom-call | flops 700000000 | bytes 5000000 | tf_op jit(solution)/shard_map/pallas_call | solution.py:327
  45.3 0.6 %copy.10 = bf16[32,1,1536]{2,0,1:T(8,128)(2,1)} copy(bf16[32,1,1536]{2,0,1:T(8,128)(2,1)S(1)} %bitcast.1) | data formatting | bytes 196608

commit v5 on v4

--- a/solution.py
+++ b/solution.py
@@ -293,9 +293,9 @@
     loads[2].wait()
     loads[3].wait()
     forward(0)
-    forward(1)
     near(0)
     ffn(0, 0, 5)
+    forward(1)
     scatter_near(0)
     near(1)
     ffn(1, 0, 5)

time: 46 us -> 46 us (level)
  no operation moved by 1% of the time
where the time goes in v5:
time: 46 us; the launch traced here: 45.9 us
  Pallas kernels  45.3 us (98%)
  local copies, waits for them, and re-layouts  0.64 us (1%)
    pallas_call x1, Pallas kernels, local(): pl.pallas_call(kernel, out_shape=pltpu.VMEM((REQ_DEV, WIDTH), bf16), in_s...  45.3 us

profile of v5, /device:TPU:16, one launch (start us, length us, event | category | flops | bytes accessed | tf_op | source)
XLA Modules:
  0.0 45.9 jit_solution(15005768021475962499)
XLA Ops:
  0.0 45.3 %shard_map.82 = bf16[32,1536]{1,0:T(8,128)(2,1)S(1)} custom-call(s32[512]{0:T(512)} %len_hbm.1, bf16[32,48]{1,0:T(8,128)(2,1)} %q_hbm.1, f32[1536]{0:T(1024)} %mix_hbm.1, f32[1536]{0:T(1024)} %gain_hbm.1, bf16[96,48,128]{2,1,0:T(8,128)(2,1)} %k_hbm.1, bf16[96,48,128]{2,1,0:T(8,128)(2,1)} %v_hbm.1, bf16[1,1536,384]{2,1,0:T(8,128)(2,1)} %up_hbm.1, ...), custom_call_target="tpu_custom_call" | custom-call | flops 700000000 | bytes 5000000 | tf_op jit(solution)/shard_map/pallas_call | solution.py:327
  45.3 0.6 %copy.10 = bf16[32,1,1536]{2,0,1:T(8,128)(2,1)} copy(bf16[32,1,1536]{2,0,1:T(8,128)(2,1)S(1)} %bitcast.1) | data formatting | bytes 196608

commit v6 on v4

--- a/solution.py
+++ b/solution.py
@@ -297,14 +297,14 @@
     near(0)
     ffn(0, 0, 5)
     scatter_near(0)
-    near(1)
-    ffn(1, 0, 5)
     far(0)
     ffn(0, 5, 8)
     scatter(0)
     far(1)
     ffn(1, 5, 8)
     scatter(1)
+    near(1)
+    ffn(1, 0, 5)
     scatter_near(1)
     relay(0)
     relay(1)

time: 46 us -> 46 us (level)
  no operation moved by 1% of the time
where the time goes in v6:
time: 46 us; the launch traced here: 45.9 us
  Pallas kernels  45.3 us (98%)
  local copies, waits for them, and re-layouts  0.64 us (1%)
    pallas_call x1, Pallas kernels, local(): pl.pallas_call(kernel, out_shape=pltpu.VMEM((REQ_DEV, WIDTH), bf16), in_s...  45.3 us

profile of v6, /device:TPU:16, one launch (start us, length us, event | category | flops | bytes accessed | tf_op | source)
XLA Modules:
  0.0 45.9 jit_solution(1870384362077264096)
XLA Ops:
  0.0 45.3 %shard_map.82 = bf16[32,1536]{1,0:T(8,128)(2,1)S(1)} custom-call(s32[512]{0:T(512)} %len_hbm.1, bf16[32,48]{1,0:T(8,128)(2,1)} %q_hbm.1, f32[1536]{0:T(1024)} %mix_hbm.1, f32[1536]{0:T(1024)} %gain_hbm.1, bf16[96,48,128]{2,1,0:T(8,128)(2,1)} %k_hbm.1, bf16[96,48,128]{2,1,0:T(8,128)(2,1)} %v_hbm.1, bf16[1,1536,384]{2,1,0:T(8,128)(2,1)} %up_hbm.1, ...), custom_call_target="tpu_custom_call" | custom-call | flops 700000000 | bytes 5000000 | tf_op jit(solution)/shard_map/pallas_call | solution.py:327
  45.3 0.6 %copy.10 = bf16[32,1,1536]{2,0,1:T(8,128)(2,1)} copy(bf16[32,1,1536]{2,0,1:T(8,128)(2,1)S(1)} %bitcast.1) | data formatting | bytes 196608
